TPU v7x, 32 devices: a whole 2x2x4 slice. The times are simulated.
32 devices in a mesh: groups: 2 (over y), dp: 4 (over x, core), tok: 4 (over z).
Axes of the slice: x: 2, y: 2, z: 4, core: 2. Of those that a mesh axis runs over, the one named last changes fastest.
Arguments:
- train_inputs: bfloat16 [8, 1024, 8192], P(('groups', 'dp'), 'tok'), parts along dimension 0, may hold values from -6 to 6
- train_grads: bfloat16 [8, 1024, 8192], P(('groups', 'dp'), 'tok'), parts along dimension 0, may hold values from -6 to 6
- query_inputs: bfloat16 [16, 1024, 8192], P(('groups', 'dp'), 'tok'), parts along dimension 0, may hold values from -6 to 6
- query_grads: bfloat16 [16, 1024, 8192], P(('groups', 'dp'), 'tok'), parts along dimension 0, may hold values from -6 to 6
- proj_in: bfloat16 [128, 8192], replicated, may hold values from -0.0625 to 0.0625
- proj_out: bfloat16 [128, 8192], replicated, may hold values from -0.0625 to 0.0625
- left_factor: float32 [128, 128], replicated, may hold values from -0.5 to 0.5
- right_factor: float32 [128, 128], replicated, may hold values from -0.5 to 0.5
- train_lengths: int32 [8], P(('groups', 'dp')), parts along dimension 0, may hold values from 128 to 1024, as said below
- train_mask: int32 [8, 1024], P(('groups', 'dp'), 'tok'), parts along dimension 0, may hold values 0 or 1
- query_lengths: int32 [16], P(('groups', 'dp')), parts along dimension 0, may hold values from 128 to 1024, as said below
- query_mask: int32 [16, 1024], P(('groups', 'dp'), 'tok'), parts along dimension 0, may hold values 0 or 1
Outputs:
- scores: float32 [8, 8], P(None, ('groups', 'dp')), parts along dimension 1
There are 2 independent parts, one for each index of `groups`. A program takes and returns all parts, laid end to end along the dimension named above; an argument that names none is the same for every part. Nothing has to cross between parts.
Inputs may be any that keep to these rules, and one draw needn't show every extreme that they name: `train_lengths`: at least one transcript is 1024 long and at least one is 128 long. `query_lengths`: at least one transcript is 1024 long and at least one is 128 long.
All inputs are finite; a program needn't handle non-finite values. No bound on the sum of `train_mask` or of `query_mask` on one device may be relied on, other than what follows from the above.
Results may differ from a plain program's by a relative error of at most 0.0003.
Values sent between devices are 32-bit elements; how exact they have to be, the bound alone decides.
A program may use at most 128 MiB of HBM per device.

v0:
```python
import jax
import jax.numpy as jnp
from jax import lax
from jax.sharding import PartitionSpec as P


def weighted_sketch(in_proj, out_proj, lengths, mask):
    tok_rows = mask.shape[1]
    positions = lax.axis_index("tok") * tok_rows + jnp.arange(tok_rows, dtype=jnp.int32)
    weight = (mask * (positions[None, :] < lengths[:, None]).astype(jnp.int32)).astype(jnp.float32)
    total = jnp.einsum(
        "etk,etj->ekj", out_proj * weight[:, :, None], in_proj, precision=lax.Precision.HIGHEST
    )
    return total / jnp.sqrt(lengths.astype(jnp.float32))[:, None, None]


def per_device(
    train_inputs,
    train_grads,
    query_inputs,
    query_grads,
    proj_in,
    proj_out,
    left_factor,
    right_factor,
    train_lengths,
    train_mask,
    query_lengths,
    query_mask,
):
    sketch_size = proj_in.shape[0]
    train_in = jnp.einsum("etd,kd->etk", train_inputs, proj_in, preferred_element_type=jnp.float32)
    train_out = jnp.einsum("etd,kd->etk", train_grads, proj_out, preferred_element_type=jnp.float32)
    query_in = jnp.einsum("etd,kd->etk", query_inputs, proj_in, preferred_element_type=jnp.float32)
    query_out = jnp.einsum("etd,kd->etk", query_grads, proj_out, preferred_element_type=jnp.float32)
    train_part = weighted_sketch(train_in, train_out, train_lengths, train_mask)
    query_part = weighted_sketch(query_in, query_out, query_lengths, query_mask)
    leftside = jnp.matmul(left_factor, query_part, precision=lax.Precision.HIGHEST)
    query_precond = jnp.matmul(leftside, right_factor, precision=lax.Precision.HIGHEST)
    train_flat = train_part.reshape(train_part.shape[0], sketch_size * sketch_size)
    query_flat = query_precond.reshape(query_precond.shape[0], sketch_size * sketch_size)
    train_total, query_total = lax.psum((train_flat, query_flat), "tok")
    return (
        jnp.dot(
            lax.all_gather(query_total, "dp", axis=0, tiled=True),
            train_total.T,
            precision=lax.Precision.HIGHEST,
        )
        / sketch_size
    )


def solution(mesh):
    return jax.shard_map(
        per_device,
        mesh=mesh,
        in_specs=(
            P(("groups", "dp"), "tok", None),
            P(("groups", "dp"), "tok", None),
            P(("groups", "dp"), "tok", None),
            P(("groups", "dp"), "tok", None),
            P(),
            P(),
            P(),
            P(),
            P(("groups", "dp")),
            P(("groups", "dp"), "tok"),
            P(("groups", "dp")),
            P(("groups", "dp"), "tok"),
        ),
        out_specs=P(None, ("groups", "dp")),
        check_vma=False,
    )
```

profile of v0, /device:TPU:0, one launch (start us, length us, event | category | flops | bytes accessed | tf_op | source)
XLA Modules:
  0.0 79.3 jit_solution(4102055950789656058)
XLA Ops:
  7.4 0.7 convert_sqrt_fusion
  8.1 0.1 copy-done
  8.1 3.6 %fusion = f32[256,128]{1,0:T(8,128)S(1)} fusion(bf16[128,8192]{1,0:T(8,128)(2,1)S(1)} %copy-done, bf16[1,256,8192]{2,1,0:T(8,128)(2,1)} %param.12), kind=kOutput, calls=%fused_computation | convolution fusion | flops 536870912 | bytes 6422528 | tf_op jit(solution)/shard_map/etd,kd->etk/dot_general | solution.py:32
  11.7 0.0 copy-start.5
  11.7 0.0 copy-start.7
  11.8 0.0 copy-start.2
  11.8 0.0 slice-start.1
  11.8 5.9 %fusion.4 = f32[2,256,128]{2,1,0:T(8,128)S(1)} fusion(bf16[2,256,8192]{2,1,0:T(8,128)(2,1)} %param.14, bf16[128,8192]{1,0:T(8,128)(2,1)S(1)} %copy-done), kind=kOutput, calls=%fused_computation.4 | convolution fusion | flops 1073741824 | bytes 10747904 | tf_op jit(solution)/shard_map/etd,kd->etk/dot_general | solution.py:34
  17.7 0.1 fusion.19
  17.8 0.0 copy-start.3
  17.8 0.0 copy-start.6
  17.8 0.0 copy-start.1
  17.8 2.3 %fusion.8 = f32[2,256,128]{2,1,0:T(8,128)S(1)} fusion(bf16[2,256,8192]{2,1,0:T(8,128)(2,1)S(1)} %bitcast.62, bf16[128,8192]{1,0:T(8,128)(2,1)S(1)} %copy-done.2, f32[2,256]{1,0:T(2,128)S(1)} %fusion.19), kind=kOutput, calls=%fused_computation.8 | convolution fusion | flops 1073807360 | bytes 10749952 | tf_op jit(solution)/shard_map/etd,kd->etk/dot_general | solution.py:35
  20.2 0.6 convolution_divide_fusion
  20.8 0.3 convolution_bitcast_fusion.1
  21.1 0.3 convolution_bitcast_fusion
  21.4 0.8 copy.15
  22.1 1.2 %fusion.11 = f32[256,128]{1,0:T(8,128)S(1)} fusion(bf16[128,8192]{1,0:T(8,128)(2,1)S(1)} %copy-done.2, bf16[1,256,8192]{2,1,0:T(8,128)(2,1)S(1)} %copy-done.1, f32[256]{0:T(256)S(1)} %bitcast.60), kind=kOutput, calls=%fused_computation.9 | convolution fusion | flops 536903680 | bytes 6423552 | tf_op jit(solution)/shard_map/etd,kd->etk/dot_general | solution.py:33
  23.4 1.0 %fusion.14 = f32[16384]{0:T(1024)} fusion(f32[256,128]{1,0:T(8,128)S(1)} %fusion.11, f32[256,128]{1,0:T(8,128)S(1)} %fusion, f32[]{:T(128)} %bitcast.10), kind=kOutput, calls=%fused_computation.14 | convolution fusion | flops 50348032 | bytes 327684 | tf_op jit(solution)/shard_map/etk,etj->ekj/dot_general | solution.py:11
  24.4 0.0 all-reduce.3.cloned.1.call-update
  24.4 37.7 %all-reduce.3.cloned.1.call-done = (f32[2,16384]{1,0:T(2,128)}, f32[16384]{0:T(1024)}) async-done(((f32[2,16384]{1,0:T(2,128)}, f32[16384]{0:T(1024)}), (f32[2,16384]{1,0:T(2,128)}, f32[16384]{0:T(1024)})) %all-reduce.3.cloned.1.call-update) | async-done | bytes 196624 | tf_op jit(solution)/shard_map/psum | solution.py:42
  62.1 7.3 %all-gather = f32[4,2,16384]{2,1,0:T(2,128)S(1)} all-gather(f32[1,2,16384]{2,1,0:T(2,128)} %bitcast.58), channel_id=1, replica_groups=mesh['groups'=2,'dp'=4,'tok'=4] {'dp'}, dimensions={0}, use_global_device_ids=true | all-gather | bytes 655360 | tf_op jit(solution)/shard_map/all_gather | solution.py:45
  69.5 0.4 reshape.60
  69.8 2.6 %fusion.16 = f32[8,1]{0,1:T(1,128)} fusion(f32[8,16384]{1,0:T(8,128)S(1)} %reshape.60, f32[16384,1]{0,1:T(1,128)} %bitcast.59), kind=kOutput, calls=%fused_computation.17 | convolution fusion | flops 1572872 | bytes 589856 | tf_op jit(solution)/shard_map/dot_general | solution.py:44
  (16 shorter events, 0.0 us)
Async XLA Ops:
  6.5 1.6 %copy-start = (bf16[128,8192]{1,0:T(8,128)(2,1)S(1)}, bf16[128,8192]{1,0:T(8,128)(2,1)}, u32[]{:S(2)}) copy-start(bf16[128,8192]{1,0:T(8,128)(2,1)} %param.16) | copy-start | bytes 6291460
  6.5 55.6 %all-reduce.3.cloned.1.call-start = ((), (), s32[]{:S(2)}) async-start(), calls=%async_computation | async-start | bytes 393216 | tf_op jit(solution)/shard_map/psum | solution.py:42
  8.1 9.6 %slice-start = ((s8[8388608]{0:T(1024)(128)(4,1)}), s8[4194304]{0:T(1024)(128)(4,1)S(1)}, s32[]{:S(2)}) async-start(s8[8388608]{0:T(1024)(128)(4,1)} %bitcast.61), calls=%async_computation.1 | async-start | bytes 8388608
  11.7 5.9 %copy-start.5 = (s32[2,256]{1,0:T(2,128)S(1)}, s32[2,256]{1,0:T(2,128)}, u32[]{:S(2)}) copy-start(s32[2,256]{1,0:T(2,128)} %param.23) | copy-start | bytes 6148
  11.7 5.9 %copy-start.7 = (s32[2]{0:T(128)S(1)}, s32[2]{0:T(128)}, u32[]{:S(2)}) copy-start(s32[2]{0:T(128)} %param.22) | copy-start | bytes 28
  11.8 6.0 %copy-start.2 = (bf16[128,8192]{1,0:T(8,128)(2,1)S(1)}, bf16[128,8192]{1,0:T(8,128)(2,1)}, u32[]{:S(2)}) copy-start(bf16[128,8192]{1,0:T(8,128)(2,1)} %param.17) | copy-start | bytes 6291460
  11.8 6.0 %slice-start.1 = ((s8[8388608]{0:T(1024)(128)(4,1)}), s8[4194304]{0:T(1024)(128)(4,1)S(1)}, s32[]{:S(2)}) async-start(s8[8388608]{0:T(1024)(128)(4,1)} %bitcast.61), calls=%async_computation.2 | async-start | bytes 8388608
  17.8 3.0 %copy-start.3 = (f32[128,128]{1,0:T(8,128)S(1)}, f32[128,128]{1,0:T(8,128)}, u32[]{:S(2)}) copy-start(f32[128,128]{1,0:T(8,128)} %param.18) | copy-start | bytes 196612
  17.8 3.3 %copy-start.4 = (f32[128,128]{1,0:T(8,128)S(1)}, f32[128,128]{1,0:T(8,128)}, u32[]{:S(2)}) copy-start(f32[128,128]{1,0:T(8,128)} %param.19) | copy-start | bytes 196612
  17.8 4.3 %copy-start.6 = (s32[1,256]{1,0:T(1,128)S(1)}, s32[1,256]{1,0:T(1,128)}, u32[]{:S(2)}) copy-start(s32[1,256]{1,0:T(1,128)} %param.21) | copy-start | bytes 3076
  17.8 4.3 %copy-start.1 = (bf16[1,256,8192]{2,1,0:T(8,128)(2,1)S(1)}, bf16[1,256,8192]{2,1,0:T(8,128)(2,1)}, u32[]{:S(2)}) copy-start(bf16[1,256,8192]{2,1,0:T(8,128)(2,1)} %param.13) | copy-start | bytes 12582916
Sparse Core Ops, SparseCore 0:
  24.6 37.5 all-reduce.2
where the time goes:
time: 79.5 us; the launch traced here: 79.3 us
  waiting for transfers between devices  37.7 us (47%)
  matrix products  17.8 us (22%)
  between operations  14.4 us (18%)
  blocking collectives  7.34 us (9%)
  local copies, waits for them, and re-layouts  1.25 us (2%)
    psum x1, waiting for transfers between devices, per_device(): train_total, query_total = lax.psum((train_flat, query_flat), 'tok')  37.7 us
    all_gather x1, blocking collectives, per_device(): lax.all_gather(query_total, 'dp', axis=0, tiled=True)  7.34 us
    dot_general x1, matrix products, per_device(): jnp.einsum('etd,kd->etk', query_inputs, proj_in, preferred_element_type=j...  5.87 us
    dot_general x1, matrix products, per_device(): jnp.einsum('etd,kd->etk', train_inputs, proj_in, preferred_element_type=j...  3.58 us
    dot_general x1, matrix products, per_device(): jnp.dot(lax.all_gather(query_total, 'dp', axis=0, tiled=True), train_tota...  2.59 us
    dot_general x1, matrix products, per_device(): jnp.einsum('etd,kd->etk', query_grads, proj_out, preferred_element_type=j...  2.34 us
    dot_general x2, matrix products, weighted_sketch(): jnp.einsum('etk,etj->ekj', out_proj * weight[:, :, None], in_proj, precis...  1.66 us
  transfers between devices with their start and end apart: 1, of which 1 were waited for; matrix products, arithmetic and copies ran while one was open for 0% of the time, Pallas kernels for 0%

commit v1 on v0

v1 whole, which is shorter than its diff:
```python
import functools

import jax
import jax.numpy as jnp
from jax import lax
from jax.experimental import pallas as pl
from jax.experimental.pallas import tpu as pltpu
from jax.sharding import PartitionSpec as P

CHUNKS = 8
MESH = pl.DeviceIdType.MESH
HIGHEST = lax.Precision.HIGHEST


def dot_nt(a, b, precision=None):
    return lax.dot_general(
        a, b, (((1,), (1,)), ((), ())), precision=precision, preferred_element_type=jnp.float32
    )


def kernel(
    n_dp,
    n_tok,
    train_in_hbm,
    train_grad_hbm,
    query_in_hbm,
    query_grad_hbm,
    proj_in_hbm,
    proj_out_hbm,
    left_ref,
    right_ref,
    train_len_ref,
    train_mask_ref,
    query_len_ref,
    query_mask_ref,
    out_ref,
    train_in,
    train_grad,
    query_in,
    query_grad,
    proj_in,
    proj_out,
    acc_a,
    acc_b,
    acc_q,
    weighted,
    part,
    scattered,
    precond,
    own_scores,
    all_scores,
    load_sem,
    scatter_send,
    scatter_recv,
    gather_send,
    gather_recv,
    core_send,
    core_recv,
    score_send,
    score_recv,
):
    n_dev = n_dp * n_tok
    n_half = n_dev // 2
    n_query, tok_rows, width = query_in.shape
    size = proj_in.shape[0]
    cols = width // CHUNKS
    dp, tok = lax.axis_index("dp"), lax.axis_index("tok")
    core, pair = lax.rem(dp, 2), lax.div(dp, 2)
    me = dp * n_tok + tok

    def loads(kind, c):
        span = pl.ds(c * cols, cols)
        pairs = {
            0: (proj_in_hbm.at[:, span], proj_in.at[:, span]),
            1: (train_in_hbm.at[0, :, span], train_in.at[:, span]),
            2: (proj_out_hbm.at[:, span], proj_out.at[:, span]),
            3: (train_grad_hbm.at[0, :, span], train_grad.at[:, span]),
            4: (query_grad_hbm.at[:, :, span], query_grad.at[:, :, span]),
            5: (query_in_hbm.at[:, :, span], query_in.at[:, :, span]),
        }
        return pltpu.make_async_copy(*pairs[kind], load_sem.at[kind, c])

    for c in range(CHUNKS):
        for kind in range(4):
            loads(kind, c).start()
    for kind in (4, 5):
        for c in range(CHUNKS):
            loads(kind, c).start()

    barrier = pltpu.get_barrier_semaphore()
    unroll = n_dev <= 16

    def greet(i, carry):
        other = lax.rem(me + i, n_dev)
        pl.semaphore_signal(
            barrier,
            inc=1,
            device_id={"dp": lax.div(other, n_tok), "tok": lax.rem(other, n_tok)},
            device_id_type=MESH,
        )
        return carry

    lax.fori_loop(1, n_dev, greet, 0, unroll=unroll)

    positions = tok * tok_rows + lax.broadcasted_iota(jnp.int32, (1, tok_rows), 1)

    def weight(mask_row, length):
        lengths = jnp.full((1, tok_rows), length, jnp.int32)
        valid = (mask_row * (positions < lengths).astype(jnp.int32)).astype(jnp.float32)
        return valid / jnp.sqrt(lengths.astype(jnp.float32))

    for c in range(CHUNKS):
        span = pl.ds(c * cols, cols)
        for kind, rows, proj, acc in ((0, train_in, proj_in, acc_a), (2, train_grad, proj_out, acc_b)):
            loads(kind, c).wait()
            loads(kind + 1, c).wait()
            term = dot_nt(rows[:, span], proj[:, span])
            if c == 0:
                acc[...] = term
            else:
                acc[...] += term
    out_t = jnp.transpose(acc_b[...]) * (weight(train_mask_ref[0:1, :], train_len_ref[0]) * (1.0 / size))
    sketch = jnp.dot(out_t, acc_a[...], precision=HIGHEST, preferred_element_type=jnp.float32)
    leftside = jnp.dot(
        jnp.transpose(left_ref[...]), sketch, precision=HIGHEST, preferred_element_type=jnp.float32
    )
    part[...] = dot_nt(leftside, right_ref[...], HIGHEST).reshape(part.shape)

    pl.semaphore_wait(barrier, n_dev - 1)

    def scatter_copy(i):
        other = lax.rem(tok + i, n_tok)
        return pltpu.make_async_remote_copy(
            src_ref=part.at[other],
            dst_ref=scattered.at[tok],
            send_sem=scatter_send,
            recv_sem=scatter_recv,
            device_id={"tok": other},
            device_id_type=MESH,
        )

    for i in range(1, n_tok):
        scatter_copy(i).start()
    scattered[pl.ds(tok, 1)] = part[pl.ds(tok, 1)]

    def bulk(ref, count, send, recv):
        return pltpu.make_async_remote_copy(
            src_ref=ref.at[pl.ds(0, count)],
            dst_ref=ref.at[pl.ds(0, count)],
            send_sem=send,
            recv_sem=recv,
            device_id={"dp": dp},
            device_id_type=MESH,
        )

    def gather_start():
        bulk(scattered, n_tok - 1, scatter_send, scatter_recv).wait_recv()
        precond[pl.ds(me, 1)] = jnp.sum(scattered[...], axis=0, keepdims=True)

        def send(i, carry):
            other = lax.rem(pair * n_tok + tok + i, n_half)
            pltpu.make_async_remote_copy(
                src_ref=precond.at[me],
                dst_ref=precond.at[me],
                send_sem=gather_send,
                recv_sem=gather_recv,
                device_id={"dp": 2 * lax.div(other, n_tok) + core, "tok": lax.rem(other, n_tok)},
                device_id_type=MESH,
            ).start()
            return carry

        lax.fori_loop(1, n_half, send, 0, unroll=unroll)

    def core_start():
        bulk(precond, n_half - 1, gather_send, gather_recv).wait_recv()
        for p in range(n_dp // 2):
            block = precond.at[pl.ds((2 * p + core) * n_tok, n_tok)]
            pltpu.make_async_remote_copy(
                src_ref=block,
                dst_ref=block,
                send_sem=core_send,
                recv_sem=core_recv,
                device_id={"dp": 2 * pair + 1 - core},
                device_id_type=MESH,
            ).start()

    for c in range(CHUNKS):
        span = pl.ds(c * cols, cols)
        loads(4, c).wait()
        term = dot_nt(query_grad[:, :, span].reshape(n_query * tok_rows, cols), proj_out[:, span])
        if c == 0:
            acc_q[...] = term
        else:
            acc_q[...] += term
        if c == 5:
            gather_start()
    for j in range(n_query):
        weighted[j] = jnp.transpose(acc_q[pl.ds(j * tok_rows, tok_rows), :]) * weight(
            query_mask_ref[j : j + 1, :], query_len_ref[j]
        )
    for c in range(CHUNKS):
        span = pl.ds(c * cols, cols)
        loads(5, c).wait()
        term = dot_nt(query_in[:, :, span].reshape(n_query * tok_rows, cols), proj_in[:, span])
        if c == 0:
            acc_q[...] = term
        else:
            acc_q[...] += term
    core_start()
    sketches = [
        jnp.dot(
            weighted[j],
            acc_q[pl.ds(j * tok_rows, tok_rows), :],
            precision=HIGHEST,
            preferred_element_type=jnp.float32,
        )
        for j in range(n_query)
    ]
    bulk(precond, n_half, core_send, core_recv).wait_recv()
    for n in range(n_dp):
        block = precond[pl.ds(n * n_tok, n_tok)].reshape(size, size)
        for j in range(n_query):
            own_scores[n, j : j + 1, :] = jnp.sum(sketches[j] * block, axis=0, keepdims=True)

    def send_scores(i, carry):
        other = lax.rem(me + i, n_dev)
        to_dp, to_tok = lax.div(other, n_tok), lax.rem(other, n_tok)
        pltpu.make_async_remote_copy(
            src_ref=own_scores.at[to_dp],
            dst_ref=all_scores.at[me],
            send_sem=score_send,
            recv_sem=score_recv,
            device_id={"dp": to_dp, "tok": to_tok},
            device_id_type=MESH,
        ).start()
        return carry

    lax.fori_loop(1, n_dev, send_scores, 0, unroll=unroll)
    all_scores[pl.ds(me, 1)] = own_scores[pl.ds(dp, 1)]
    bulk(all_scores, n_dev - 1, score_send, score_recv).wait_recv()
    for d in range(n_dp):
        out_ref[pl.ds(d * n_query, n_query), :] = jnp.sum(all_scores[pl.ds(d * n_tok, n_tok)], axis=0)

    bulk(scattered, n_tok - 1, scatter_send, scatter_recv).wait_send()
    bulk(precond, n_half - 1, gather_send, gather_recv).wait_send()
    bulk(precond, n_half, core_send, core_recv).wait_send()
    bulk(all_scores, n_dev - 1, score_send, score_recv).wait_send()


def per_device(n_dp, n_tok, *args):
    train_inputs, query_inputs, proj_in = args[0], args[2], args[4]
    _, tok_rows, width = train_inputs.shape
    n_query = query_inputs.shape[0]
    size = proj_in.shape[0]
    n_dev = n_dp * n_tok
    rows = size // n_tok
    hbm = pl.BlockSpec(memory_space=pl.ANY)
    vmem = pl.BlockSpec(memory_space=pltpu.VMEM)
    smem = pl.BlockSpec(memory_space=pltpu.SMEM)
    dma = pltpu.SemaphoreType.DMA
    lanes = pl.pallas_call(
        functools.partial(kernel, n_dp, n_tok),
        out_shape=jax.ShapeDtypeStruct((n_dp * n_query, size), jnp.float32),
        in_specs=[hbm] * 6 + [vmem, vmem, smem, vmem, smem, vmem],
        out_specs=vmem,
        scratch_shapes=[
            pltpu.VMEM((tok_rows, width), jnp.bfloat16),
            pltpu.VMEM((tok_rows, width), jnp.bfloat16),
            pltpu.VMEM((n_query, tok_rows, width), jnp.bfloat16),
            pltpu.VMEM((n_query, tok_rows, width), jnp.bfloat16),
            pltpu.VMEM((size, width), jnp.bfloat16),
            pltpu.VMEM((size, width), jnp.bfloat16),
            pltpu.VMEM((tok_rows, size), jnp.float32),
            pltpu.VMEM((tok_rows, size), jnp.float32),
            pltpu.VMEM((n_query * tok_rows, size), jnp.float32),
            pltpu.VMEM((n_query, size, tok_rows), jnp.float32),
            pltpu.VMEM((n_tok, rows, size), jnp.float32),
            pltpu.VMEM((n_tok, rows, size), jnp.float32),
            pltpu.VMEM((n_dev, rows, size), jnp.float32),
            pltpu.VMEM((n_dp, n_query, size), jnp.float32),
            pltpu.VMEM((n_dev, n_query, size), jnp.float32),
            dma((6, CHUNKS)),
            dma,
            dma,
            dma,
            dma,
            dma,
            dma,
            dma,
            dma,
        ],
        compiler_params=pltpu.CompilerParams(
            collective_id=0, has_side_effects=True, vmem_limit_bytes=44 * 1024 * 1024
        ),
        cost_estimate=pl.CostEstimate(
            flops=4 * (1 + n_query) * tok_rows * width * size,
            bytes_accessed=4 * (1 + n_query) * tok_rows * width + 4 * size * width,
            transcendentals=0,
        ),
    )(*args)
    return jnp.sum(lanes, axis=1, keepdims=True)


def solution(mesh):
    n_dp, n_tok = mesh.shape["dp"], mesh.shape["tok"]
    row = P(("groups", "dp"), "tok", None)
    return jax.shard_map(
        functools.partial(per_device, n_dp, n_tok),
        mesh=mesh,
        in_specs=(
            row,
            row,
            row,
            row,
            P(),
            P(),
            P(),
            P(),
            P(("groups", "dp")),
            P(("groups", "dp"), "tok"),
            P(("groups", "dp")),
            P(("groups", "dp"), "tok"),
        ),
        out_specs=P(None, ("groups", "dp")),
        check_vma=False,
    )
```

time: 79.5 us -> 36.9 us (0.46)
  waiting for transfers between devices: 37.7 us -> 0 us
  Pallas kernels: 0 us -> 26.2 us
  matrix products: 17.8 us -> 0 us
  between operations: 14.4 us -> 0.68 us
  local copies, waits for them, and re-layouts: 1.25 us -> 9.05 us
  blocking collectives: 7.34 us -> 0 us
    psum x1 -> x0, waiting for transfers between devices: 37.7 us -> none  [per_device(): train_total, query_total = lax.psum((train_flat, query_flat), 'tok')]
    pallas_call x0 -> x1, Pallas kernels: none -> 26.2 us  [per_device(): pl.pallas_call(functools.partial(kernel, n_dp, n_tok), out_shape=jax.Shap...]
    dot_general x9 -> x0, matrix products: 17.8 us -> none  [the longest x1 5.87 us: per_device(): jnp.einsum('etd,kd->etk', query_inputs, proj_in, preferred_element_type=j...]
    unnamed x22 -> x16, local copies, waits for them, and re-layouts: 1.25 us -> 9.05 us
    all_gather x1 -> x0, blocking collectives: 7.34 us -> none  [per_device(): lax.all_gather(query_total, 'dp', axis=0, tiled=True)]
  transfers between devices with their start and end apart: 1 -> 0, of which waited for: 1 -> 0; matrix products, arithmetic and copies ran while one was open for 0% -> 0% of each run, Pallas kernels for 0% -> 0%
where the time goes in v1:
time: 36.9 us; the launch traced here: 36.5 us
  Pallas kernels  26.2 us (71%)
  local copies, waits for them, and re-layouts  9.05 us (25%)
  between operations  0.68 us (2%)
  other arithmetic  0.63 us (2%)
    pallas_call x1, Pallas kernels, per_device(): pl.pallas_call(functools.partial(kernel, n_dp, n_tok), out_shape=jax.Shap...  26.2 us
    unnamed x16, local copies, waits for them, and re-layouts  9.05 us

profile of v1, /device:TPU:0, one launch (start us, length us, event | category | flops | bytes accessed | tf_op | source)
XLA Modules:
  0.0 36.5 jit_solution(18343836137896462507)
XLA Ops:
  0.7 0.0 copy-start
  0.7 2.2 %copy-done = bf16[1,256,8192]{2,1,0:T(8,128)(2,1)S(1)} copy-done((bf16[1,256,8192]{2,1,0:T(8,128)(2,1)S(1)}, bf16[1,256,8192]{2,1,0:T(8,128)(2,1)}, u32[]{:S(2)}) %copy-start) | copy-done | bytes 4194328
  2.8 0.0 copy-start.1
  2.8 1.6 %copy-done.1 = bf16[128,8192]{1,0:T(8,128)(2,1)S(1)} copy-done((bf16[128,8192]{1,0:T(8,128)(2,1)S(1)}, bf16[128,8192]{1,0:T(8,128)(2,1)}, u32[]{:S(2)}) %copy-start.1) | copy-done | bytes 2097176
  4.4 0.0 copy-start.2
  4.4 1.6 %copy-done.2 = bf16[128,8192]{1,0:T(8,128)(2,1)S(1)} copy-done((bf16[128,8192]{1,0:T(8,128)(2,1)S(1)}, bf16[128,8192]{1,0:T(8,128)(2,1)}, u32[]{:S(2)}) %copy-start.2) | copy-done | bytes 2097176
  6.0 0.0 copy-start.3
  6.0 0.8 %copy-done.3 = f32[128,128]{1,0:T(8,128)S(1)} copy-done((f32[128,128]{1,0:T(8,128)S(1)}, f32[128,128]{1,0:T(8,128)}, u32[]{:S(2)}) %copy-start.3) | copy-done | bytes 65560
  6.9 0.0 copy-start.4
  6.9 0.8 %copy-done.4 = f32[128,128]{1,0:T(8,128)S(1)} copy-done((f32[128,128]{1,0:T(8,128)S(1)}, f32[128,128]{1,0:T(8,128)}, u32[]{:S(2)}) %copy-start.4) | copy-done | bytes 65560
  7.7 0.0 copy-start.5
  7.7 0.7 %copy-done.5 = s32[2,256]{1,0:T(2,128)S(1)} copy-done((s32[2,256]{1,0:T(2,128)S(1)}, s32[2,256]{1,0:T(2,128)}, u32[]{:S(2)}) %copy-start.5) | copy-done | bytes 2072
  8.4 0.0 copy-start.6
  8.4 0.7 %copy-done.6 = s32[1,256]{1,0:T(1,128)S(1)} copy-done((s32[1,256]{1,0:T(1,128)S(1)}, s32[1,256]{1,0:T(1,128)}, u32[]{:S(2)}) %copy-start.6) | copy-done | bytes 1048
  9.1 0.0 copy-start.7
  9.1 0.7 %copy-done.7 = s32[2]{0:T(128)S(1)} copy-done((s32[2]{0:T(128)S(1)}, s32[2]{0:T(128)}, u32[]{:S(2)}) %copy-start.7) | copy-done | bytes 32
  9.7 26.2 %shard_map.118 = f32[8,128]{1,0:T(8,128)S(1)} custom-call(bf16[1,256,8192]{2,1,0:T(8,128)(2,1)S(1)} %copy-done, bf16[1,256,8192]{2,1,0:T(8,128)(2,1)} %train_grad_hbm.1, bf16[2,256,8192]{2,1,0:T(8,128)(2,1)} %query_in_hbm.1, bf16[2,256,8192]{2,1,0:T(8,128)(2,1)} %query_grad_hbm.1, bf16[128,8192]{1,0:T(8,128)(2,1)S(1)} %copy-done.1, ...), custom_call_target="tpu_custom_call" | custom-call | flops 3221225472 | bytes 29360128 | tf_op jit(solution)/shard_map/pallas_call | solution.py:261
  35.9 0.6 %reduce_sum.9 = f32[8]{0:T(128)} reduce(f32[8,128]{1,0:T(8,128)S(1)} %shard_map.118, f32[]{:T(128)} %constant.0.clone.1), dimensions={1}, to_apply=%region_0.0 | reduce | flops 1016 | bytes 4132 | tf_op jit(solution)/shard_map/reduce_sum | solution.py:301
Async XLA Ops:
  0.7 2.2 %copy-start = (bf16[1,256,8192]{2,1,0:T(8,128)(2,1)S(1)}, bf16[1,256,8192]{2,1,0:T(8,128)(2,1)}, u32[]{:S(2)}) copy-start(bf16[1,256,8192]{2,1,0:T(8,128)(2,1)} %train_in_hbm.1) | copy-start | bytes 12582916
  2.8 1.6 %copy-start.1 = (bf16[128,8192]{1,0:T(8,128)(2,1)S(1)}, bf16[128,8192]{1,0:T(8,128)(2,1)}, u32[]{:S(2)}) copy-start(bf16[128,8192]{1,0:T(8,128)(2,1)} %proj_in_hbm.1) | copy-start | bytes 6291460
  4.4 1.6 %copy-start.2 = (bf16[128,8192]{1,0:T(8,128)(2,1)S(1)}, bf16[128,8192]{1,0:T(8,128)(2,1)}, u32[]{:S(2)}) copy-start(bf16[128,8192]{1,0:T(8,128)(2,1)} %proj_out_hbm.1) | copy-start | bytes 6291460
  6.0 0.8 %copy-start.3 = (f32[128,128]{1,0:T(8,128)S(1)}, f32[128,128]{1,0:T(8,128)}, u32[]{:S(2)}) copy-start(f32[128,128]{1,0:T(8,128)} %left_ref.1) | copy-start | bytes 196612
  6.9 0.8 %copy-start.4 = (f32[128,128]{1,0:T(8,128)S(1)}, f32[128,128]{1,0:T(8,128)}, u32[]{:S(2)}) copy-start(f32[128,128]{1,0:T(8,128)} %right_ref.1) | copy-start | bytes 196612
  7.7 0.7 %copy-start.5 = (s32[2,256]{1,0:T(2,128)S(1)}, s32[2,256]{1,0:T(2,128)}, u32[]{:S(2)}) copy-start(s32[2,256]{1,0:T(2,128)} %query_mask_ref.1) | copy-start | bytes 6148
  8.4 0.7 %copy-start.6 = (s32[1,256]{1,0:T(1,128)S(1)}, s32[1,256]{1,0:T(1,128)}, u32[]{:S(2)}) copy-start(s32[1,256]{1,0:T(1,128)} %train_mask_ref.1) | copy-start | bytes 3076
  9.1 0.7 %copy-start.7 = (s32[2]{0:T(128)S(1)}, s32[2]{0:T(128)}, u32[]{:S(2)}) copy-start(s32[2]{0:T(128)} %query_len_ref.1) | copy-start | bytes 28

commit v2 on v1

--- a/solution.py
+++ b/solution.py
@@ -7,7 +7,8 @@
 from jax.experimental.pallas import tpu as pltpu
 from jax.sharding import PartitionSpec as P
 
-CHUNKS = 8
+CHUNKS = 4
+WINDOW = 6
 MESH = pl.DeviceIdType.MESH
 HIGHEST = lax.Precision.HIGHEST
 
@@ -27,12 +28,12 @@
     query_grad_hbm,
     proj_in_hbm,
     proj_out_hbm,
-    left_ref,
-    right_ref,
-    train_len_ref,
-    train_mask_ref,
-    query_len_ref,
-    query_mask_ref,
+    left_hbm,
+    right_hbm,
+    train_len_hbm,
+    train_mask_hbm,
+    query_len_hbm,
+    query_mask_hbm,
     out_ref,
     train_in,
     train_grad,
@@ -49,7 +50,14 @@
     precond,
     own_scores,
     all_scores,
+    left_ref,
+    right_ref,
+    train_len_ref,
+    train_mask_ref,
+    query_len_ref,
+    query_mask_ref,
     load_sem,
+    small_sem,
     scatter_send,
     scatter_recv,
     gather_send,
@@ -80,12 +88,32 @@
         }
         return pltpu.make_async_copy(*pairs[kind], load_sem.at[kind, c])
 
-    for c in range(CHUNKS):
-        for kind in range(4):
-            loads(kind, c).start()
-    for kind in (4, 5):
-        for c in range(CHUNKS):
-            loads(kind, c).start()
+    order = [(kind, c) for c in range(CHUNKS) for kind in range(4)]
+    order += [(4, c) for c in range(CHUNKS)] + [(5, c) for c in range(CHUNKS)]
+    for load in order[:WINDOW]:
+        loads(*load).start()
+
+    def fetch(*load):
+        loads(*load).wait()
+        ahead = order.index(load) + WINDOW
+        if ahead < len(order):
+            loads(*order[ahead]).start()
+
+    small = [
+        pltpu.make_async_copy(src, dst, small_sem.at[i])
+        for i, (src, dst) in enumerate(
+            (
+                (left_hbm, left_ref),
+                (right_hbm, right_ref),
+                (train_len_hbm, train_len_ref),
+                (train_mask_hbm, train_mask_ref),
+                (query_len_hbm, query_len_ref),
+                (query_mask_hbm, query_mask_ref),
+            )
+        )
+    ]
+    for copy in small:
+        copy.start()
 
     barrier = pltpu.get_barrier_semaphore()
     unroll = n_dev <= 16
@@ -112,15 +140,17 @@
     for c in range(CHUNKS):
         span = pl.ds(c * cols, cols)
         for kind, rows, proj, acc in ((0, train_in, proj_in, acc_a), (2, train_grad, proj_out, acc_b)):
-            loads(kind, c).wait()
-            loads(kind + 1, c).wait()
-            term = dot_nt(rows[:, span], proj[:, span])
+            fetch(kind, c)
+            fetch(kind + 1, c)
+            term = dot_nt(proj[:, span], rows[:, span])
             if c == 0:
                 acc[...] = term
             else:
                 acc[...] += term
-    out_t = jnp.transpose(acc_b[...]) * (weight(train_mask_ref[0:1, :], train_len_ref[0]) * (1.0 / size))
-    sketch = jnp.dot(out_t, acc_a[...], precision=HIGHEST, preferred_element_type=jnp.float32)
+    for copy in small:
+        copy.wait()
+    out_t = acc_b[...] * (weight(train_mask_ref[0:1, :], train_len_ref[0]) * (1.0 / size))
+    sketch = dot_nt(out_t, acc_a[...], HIGHEST)
     leftside = jnp.dot(
         jnp.transpose(left_ref[...]), sketch, precision=HIGHEST, preferred_element_type=jnp.float32
     )
@@ -186,34 +216,29 @@
 
     for c in range(CHUNKS):
         span = pl.ds(c * cols, cols)
-        loads(4, c).wait()
-        term = dot_nt(query_grad[:, :, span].reshape(n_query * tok_rows, cols), proj_out[:, span])
+        fetch(4, c)
+        term = dot_nt(proj_out[:, span], query_grad[:, :, span].reshape(n_query * tok_rows, cols))
         if c == 0:
             acc_q[...] = term
         else:
             acc_q[...] += term
-        if c == 5:
+        if c == 3:
             gather_start()
     for j in range(n_query):
-        weighted[j] = jnp.transpose(acc_q[pl.ds(j * tok_rows, tok_rows), :]) * weight(
+        weighted[j] = acc_q[:, pl.ds(j * tok_rows, tok_rows)] * weight(
             query_mask_ref[j : j + 1, :], query_len_ref[j]
         )
     for c in range(CHUNKS):
         span = pl.ds(c * cols, cols)
-        loads(5, c).wait()
-        term = dot_nt(query_in[:, :, span].reshape(n_query * tok_rows, cols), proj_in[:, span])
+        fetch(5, c)
+        term = dot_nt(proj_in[:, span], query_in[:, :, span].reshape(n_query * tok_rows, cols))
         if c == 0:
             acc_q[...] = term
         else:
             acc_q[...] += term
     core_start()
     sketches = [
-        jnp.dot(
-            weighted[j],
-            acc_q[pl.ds(j * tok_rows, tok_rows), :],
-            precision=HIGHEST,
-            preferred_element_type=jnp.float32,
-        )
+        dot_nt(weighted[j], acc_q[:, pl.ds(j * tok_rows, tok_rows)], HIGHEST)
         for j in range(n_query)
     ]
     bulk(precond, n_half, core_send, core_recv).wait_recv()
@@ -254,14 +279,13 @@
     size = proj_in.shape[0]
     n_dev = n_dp * n_tok
     rows = size // n_tok
-    hbm = pl.BlockSpec(memory_space=pl.ANY)
+    hbm = pl.BlockSpec(memory_space=pltpu.HBM)
     vmem = pl.BlockSpec(memory_space=pltpu.VMEM)
-    smem = pl.BlockSpec(memory_space=pltpu.SMEM)
     dma = pltpu.SemaphoreType.DMA
     lanes = pl.pallas_call(
         functools.partial(kernel, n_dp, n_tok),
         out_shape=jax.ShapeDtypeStruct((n_dp * n_query, size), jnp.float32),
-        in_specs=[hbm] * 6 + [vmem, vmem, smem, vmem, smem, vmem],
+        in_specs=[hbm] * 12,
         out_specs=vmem,
         scratch_shapes=[
             pltpu.VMEM((tok_rows, width), jnp.bfloat16),
@@ -270,16 +294,18 @@
             pltpu.VMEM((n_query, tok_rows, width), jnp.bfloat16),
             pltpu.VMEM((size, width), jnp.bfloat16),
             pltpu.VMEM((size, width), jnp.bfloat16),
-            pltpu.VMEM((tok_rows, size), jnp.float32),
-            pltpu.VMEM((tok_rows, size), jnp.float32),
-            pltpu.VMEM((n_query * tok_rows, size), jnp.float32),
+            pltpu.VMEM((size, tok_rows), jnp.float32),
+            pltpu.VMEM((size, tok_rows), jnp.float32),
+            pltpu.VMEM((size, n_query * tok_rows), jnp.float32),
             pltpu.VMEM((n_query, size, tok_rows), jnp.float32),
             pltpu.VMEM((n_tok, rows, size), jnp.float32),
             pltpu.VMEM((n_tok, rows, size), jnp.float32),
             pltpu.VMEM((n_dev, rows, size), jnp.float32),
             pltpu.VMEM((n_dp, n_query, size), jnp.float32),
             pltpu.VMEM((n_dev, n_query, size), jnp.float32),
+            *[(pltpu.SMEM if x.ndim == 1 else pltpu.VMEM)(x.shape, x.dtype) for x in args[6:]],
             dma((6, CHUNKS)),
+            dma((6,)),
             dma,
             dma,
             dma,
@@ -290,7 +316,7 @@
             dma,
         ],
         compiler_params=pltpu.CompilerParams(
-            collective_id=0, has_side_effects=True, vmem_limit_bytes=44 * 1024 * 1024
+            collective_id=0, has_side_effects=True, vmem_limit_bytes=62 * 1024 * 1024
         ),
         cost_estimate=pl.CostEstimate(
             flops=4 * (1 + n_query) * tok_rows * width * size,

time: 36.9 us -> 27 us (0.73)
  local copies, waits for them, and re-layouts: 9.05 us -> 0 us
  Pallas kernels: 26.2 us -> 24.8 us
  other arithmetic: 0.63 us -> 1.31 us
    unnamed x16 -> x0, local copies, waits for them, and re-layouts: 9.05 us -> none
    pallas_call x1, Pallas kernels: 26.2 us -> 24.8 us  [per_device(): pl.pallas_call(functools.partial(kernel, n_dp, n_tok), out_shape=jax.Shap...]
    reduce_sum x1, other arithmetic: 0.63 us -> 1.31 us  [per_device(): return jnp.sum(lanes, axis=1, keepdims=True)]
where the time goes in v2:
time: 27 us; the launch traced here: 26.8 us
  Pallas kernels  24.8 us (92%)
  other arithmetic  1.31 us (5%)
  between operations  0.66 us (2%)
    pallas_call x1, Pallas kernels, per_device(): pl.pallas_call(functools.partial(kernel, n_dp, n_tok), out_shape=jax.Shap...  24.8 us
    reduce_sum x1, other arithmetic, per_device(): return jnp.sum(lanes, axis=1, keepdims=True)  1.31 us

profile of v2, /device:TPU:0, one launch (start us, length us, event | category | flops | bytes accessed | tf_op | source)
XLA Modules:
  0.0 26.8 jit_solution(8822583511736050835)
XLA Ops:
  0.7 24.8 %shard_map.118 = f32[8,128]{1,0:T(8,128)} custom-call(bf16[1,256,8192]{2,1,0:T(8,128)(2,1)} %train_in_hbm.1, bf16[1,256,8192]{2,1,0:T(8,128)(2,1)} %train_grad_hbm.1, bf16[2,256,8192]{2,1,0:T(8,128)(2,1)} %query_in_hbm.1, bf16[2,256,8192]{2,1,0:T(8,128)(2,1)} %query_grad_hbm.1, bf16[128,8192]{1,0:T(8,128)(2,1)} %proj_in_hbm.1, ...), custom_call_target="tpu_custom_call" | custom-call | flops 3221225472 | bytes 29360128 | tf_op jit(solution)/shard_map/pallas_call | solution.py:285
  25.5 1.3 %reduce_sum.9 = f32[8]{0:T(128)} reduce(f32[8,128]{1,0:T(8,128)} %shard_map.118, f32[]{:T(128)} %constant.0.clone.1), dimensions={1}, to_apply=%region_0.0 | reduce | flops 1016 | bytes 4132 | tf_op jit(solution)/shard_map/reduce_sum | solution.py:327
